TPU v7x, 32 devices: a whole 2x2x4 slice. The times are simulated.
32 devices in a mesh: tm: 32 (over z, y, x, core), rows: 1.
Axes of the slice: x: 2, y: 2, z: 4, core: 2. Of those that a mesh axis runs over, the one named last changes fastest.
Arguments:
- latent: bfloat16 [32, 2, 128, 512], P('tm', 'rows'), may hold values from -32 to 32
- norm_gain: float32 [512], replicated, may hold values from 0.1 to 1.9
- conv_weight: bfloat16 [27, 512, 512], P(None, 'tm'), may hold values from -0.0546875 to 0.0546875
- grad_out: bfloat16 [32, 2, 128, 512], P('tm', 'rows'), may hold values from -6 to 6
Outputs:
- refined: bfloat16 [32, 2, 128, 512], P('tm', 'rows')
- grad_latent: float32 [32, 2, 128, 512], P('tm', 'rows')
All inputs are finite; a program needn't handle non-finite values.
Results may differ from a plain program's by a relative error of at most 0.0013.
The roundings to bfloat16 on the way count: a program that leaves them out, or rounds other values in their place, can miss the bound.
Values may be sent and summed in bfloat16 or wider, within the bound.
A program may use at most 64 MiB of HBM per device.

v0:
```python
import jax
import jax.numpy as jnp
from jax import lax
from jax.sharding import PartitionSpec as P

GROUPS = 32


epsilon = 1e-06


def shifted(block, axis, distance):
    devices = range(lax.axis_size(axis))
    route = [(i - distance, i) for i in devices if i - distance in devices]
    return lax.ppermute(block, axis, route)


def with_halo(shard, sides, width):
    for axis, dim in sides:
        size, length = (lax.axis_size(axis), shard.shape[dim])
        up = [(i, (i + 1) % size) for i in range(size - 1)]
        down = [(j, i) for i, j in up]
        last = lax.slice_in_dim(shard, length - width, length, axis=dim)
        first = lax.slice_in_dim(shard, 0, width, axis=dim)
        before = lax.ppermute(last, axis, up)
        after = lax.ppermute(first, axis, down)
        shard = jnp.concatenate([before, shard, after], axis=dim)
    return shard


def grouped_view(values):
    return values.reshape(
        values.shape[0], values.shape[1] * values.shape[2], GROUPS, values.shape[3] // GROUPS
    )


def widen_columns(values):
    return jnp.pad(values, ((0, 0), (0, 0), (1, 1), (0, 0)))


def shards(latent, norm_gain, conv_weight, grad_out):
    frames_here, rows_here, columns, channels = latent.shape
    cell_count = lax.axis_size("rows") * rows_here * columns * (channels // GROUPS)
    full_weight = lax.all_gather(conv_weight, "tm", axis=1, tiled=True)
    latent_wide = latent.astype(jnp.float32)
    grouped = grouped_view(latent_wide)
    average = lax.psum(jnp.sum(grouped, axis=(1, 3)), "rows") / cell_count
    centred = grouped - average[:, None, :, None]
    spread = lax.psum(jnp.sum(centred * centred, axis=(1, 3)), "rows") / cell_count
    inverse = lax.rsqrt(spread + epsilon)
    normed_grouped = centred * inverse[:, None, :, None]
    normed = normed_grouped.reshape(latent.shape)
    scaled = normed * norm_gain
    sigmoid_value = jax.nn.sigmoid(scaled)
    activated = (scaled * sigmoid_value).astype(jnp.bfloat16)
    before_one = shifted(activated, "tm", 1)
    before_two = shifted(activated, "tm", 2)
    padded = with_halo(
        jnp.concatenate([before_two, before_one, activated], axis=0), (("rows", 1),), 1
    )
    after_one = shifted(grad_out, "tm", -1)
    after_two = shifted(grad_out, "tm", -2)
    padded_grad = with_halo(
        jnp.concatenate([grad_out, after_one, after_two], axis=0), (("rows", 1),), 1
    )
    padded = widen_columns(padded)
    padded_grad = widen_columns(padded_grad)
    conv_sum = jnp.zeros((frames_here * rows_here * columns, channels), jnp.float32)
    grad_act = jnp.zeros((frames_here * rows_here * columns, channels), jnp.float32)
    for time_tap in range(3):
        for row_tap in range(3):
            for col_tap in range(3):
                tap_weight = full_weight[time_tap * 9 + row_tap * 3 + col_tap]
                window = padded[
                    time_tap : time_tap + frames_here,
                    row_tap : row_tap + rows_here,
                    col_tap : col_tap + columns,
                ]
                conv_sum = conv_sum + jnp.dot(
                    window.reshape(-1, channels), tap_weight, preferred_element_type=jnp.float32
                )
                back_window = padded_grad[
                    2 - time_tap : 2 - time_tap + frames_here,
                    2 - row_tap : 2 - row_tap + rows_here,
                    2 - col_tap : 2 - col_tap + columns,
                ]
                grad_act = grad_act + lax.dot_general(
                    back_window.reshape(-1, channels),
                    tap_weight,
                    (((1,), (1,)), ((), ())),
                    preferred_element_type=jnp.float32,
                )
    refined = (latent_wide + conv_sum.reshape(latent.shape)).astype(jnp.bfloat16)
    grad_scaled = (
        grad_act.reshape(latent.shape) * sigmoid_value * (1.0 + scaled * (1.0 - sigmoid_value))
    )
    grad_normed = grouped_view(grad_scaled * norm_gain)
    first_sum, second_sum = lax.psum(
        (jnp.sum(grad_normed, axis=(1, 3)), jnp.sum(grad_normed * normed_grouped, axis=(1, 3))),
        "rows",
    )
    first = first_sum / cell_count
    second = second_sum / cell_count
    grad_norm_part = (
        grad_normed - first[:, None, :, None] - normed_grouped * second[:, None, :, None]
    ) * inverse[:, None, :, None]
    grad_latent = grad_out.astype(jnp.float32) + grad_norm_part.reshape(latent.shape)
    return (refined, grad_latent)


def solution(mesh):
    placed = (P("tm", "rows", None, None), P(), P(None, "tm", None), P("tm", "rows", None, None))
    return jax.shard_map(
        shards,
        mesh=mesh,
        in_specs=placed,
        out_specs=(P("tm", "rows", None, None), P("tm", "rows", None, None)),
        check_vma=False,
    )
```

profile of v0, /device:TPU:0, one launch (start us, length us, event | category | flops | bytes accessed | tf_op | source)
XLA Modules:
  0.0 180.6 jit_solution(16339672117282560949)
XLA Ops:
  7.2 0.7 all-gather.2.cloned.1.call-update
  7.9 1.3 collective-permute-start.4
  9.2 1.3 collective-permute-start.5
  10.5 1.0 convert_reduce_fusion
  11.7 1.0 constant_dynamic-update-slice_fusion.2
  12.7 10.2 %collective-permute-done.5 = bf16[1,2,128,512]{3,2,1,0:T(8,128)(2,1)S(1)} collective-permute-done((bf16[1,2,128,512]{3,2,1,0:T(8,128)(2,1)}, bf16[1,2,128,512]{3,2,1,0:T(8,128)(2,1)S(1)}, u32[]{:S(2)}, u32[]{:S(2)}) %collective-permute-start.5) | collective-permute-done | bytes 262176 | tf_op jit(solution)/shard_map/ppermute | solution.py:15
  23.0 0.6 copy-done.7
  23.6 0.7 collective-permute-start.6
  24.3 0.7 collective-permute-start.7
  25.2 1.0 fusion.31
  26.6 1.2 pad_maximum_fusion.6
  27.8 0.4 select_maximum_fusion
  28.2 1.7 fusion.87
  29.9 87.8 %all-gather.2.cloned.1.call-done = bf16[27,512,512]{2,1,0:T(8,128)(2,1)} async-done(((bf16[27,16,512]{2,1,0:T(8,128)(2,1)}), bf16[27,512,512]{2,1,0:T(8,128)(2,1)}) %all-gather.2.cloned.1.call-update) | async-done | bytes 14155792 | tf_op jit(solution)/shard_map/all_gather | solution.py:44
  117.7 1.6 fusion.59
  119.3 2.1 %fusion.41 = f32[256,512]{1,0:T(8,128)S(1)} fusion(bf16[256,512]{1,0:T(8,128)(2,1)} %bitcast.275, bf16[27,512,512]{2,1,0:T(8,128)(2,1)} %all-gather.2.cloned.1.call-done), kind=kOutput, calls=%fused_computation.80 | convolution fusion | flops 134217728 | bytes 1310720 | tf_op jit(solution)/shard_map/dot_general | solution.py:87
  121.4 2.2 %fusion.77 = f32[256,512]{1,0:T(8,128)S(1)} fusion(bf16[256,512]{1,0:T(8,128)(2,1)S(1)} %bitcast.224, bf16[27,512,512]{2,1,0:T(8,128)(2,1)} %all-gather.2.cloned.1.call-done), kind=kOutput, calls=%fused_computation.116 | convolution fusion | flops 134217728 | bytes 1310720 | tf_op jit(solution)/shard_map/dot_general | solution.py:87
  123.6 1.4 fusion.53
  125.0 1.5 fusion.35
  126.5 1.5 fusion.71
  127.9 1.5 fusion.81
  129.4 1.4 fusion.65
  130.9 1.4 fusion.47
  132.3 1.5 fusion.79
  133.8 1.5 fusion.33
  135.2 1.3 fusion.75
  136.5 0.3 fusion.73
  137.9 0.3 fusion.61
  138.9 0.3 fusion.51
  139.9 0.3 fusion.43
  141.0 0.3 fusion.83
  141.3 0.8 fusion.8
  142.1 0.3 fusion.85
  142.5 2.3 %collective-permute-start.1 = (bf16[1,2,128,512]{3,2,1,0:T(8,128)(2,1)S(1)}, bf16[1,2,128,512]{3,2,1,0:T(8,128)(2,1)S(1)}, u32[]{:S(2)}, u32[]{:S(2)}) collective-permute-start(bf16[1,2,128,512]{3,2,1,0:T(8,128)(2,1)S(1)} %get-tuple-element.60), channel_id=1, source_target_pairs={{0,1},{1,2},{2,3},{3,4},{4,5},{5,6},{6,7},{7,8},{8,9},{9,10},{10,1... | collective-permute-start | bytes 786440 | tf_op jit(solution)/shard_map/ppermute | solution.py:15
  144.8 3.4 %collective-permute-start = (bf16[1,2,128,512]{3,2,1,0:T(8,128)(2,1)S(1)}, bf16[1,2,128,512]{3,2,1,0:T(8,128)(2,1)S(1)}, u32[]{:S(2)}, u32[]{:S(2)}) collective-permute-start(bf16[1,2,128,512]{3,2,1,0:T(8,128)(2,1)S(1)} %get-tuple-element.60), channel_id=1, source_target_pairs={{0,2},{1,3},{2,4},{3,5},{4,6},{5,7},{6,8},{7,9},{8,10},{9,11},{10,... | collective-permute-start | bytes 786440 | tf_op jit(solution)/shard_map/ppermute | solution.py:15
  148.9 1.3 fusion.78
  150.3 4.3 %collective-permute-done = bf16[1,2,128,512]{3,2,1,0:T(8,128)(2,1)S(1)} collective-permute-done((bf16[1,2,128,512]{3,2,1,0:T(8,128)(2,1)S(1)}, bf16[1,2,128,512]{3,2,1,0:T(8,128)(2,1)S(1)}, u32[]{:S(2)}, u32[]{:S(2)}) %collective-permute-start) | collective-permute-done | bytes 262176 | tf_op jit(solution)/shard_map/ppermute | solution.py:15
  154.8 0.7 collective-permute-start.2
  155.5 0.9 collective-permute-start.3
  156.4 1.5 fusion.42
  157.8 1.3 fusion.60
  159.2 0.7 select_maximum_fusion.2
  160.0 0.8 fusion.88
  160.9 1.8 fusion.66
  162.8 1.3 fusion.48
  164.1 1.3 fusion.82
  171.6 1.1 fusion.11
  172.7 1.1 fusion.30
  (89 shorter events, 10.9 us)
Async XLA Ops:
  7.2 114.2 %copy-start.2 = (bf16[1,2,128,512]{3,2,1,0:T(8,128)(2,1)S(1)}, bf16[1,2,128,512]{3,2,1,0:T(8,128)(2,1)}, u32[]{:S(2)}) copy-start(bf16[1,2,128,512]{3,2,1,0:T(8,128)(2,1)} %param.7) | copy-start | bytes 786436
  7.2 110.5 %all-gather.2.cloned.1.call-start = ((), (), s32[]{:S(2)}) async-start(), calls=%async_computation | async-start | bytes 14598144 | tf_op jit(solution)/shard_map/all_gather | solution.py:44
  7.9 4.8 %collective-permute-start.4 = (bf16[1,2,128,512]{3,2,1,0:T(8,128)(2,1)}, bf16[1,2,128,512]{3,2,1,0:T(8,128)(2,1)S(1)}, u32[]{:S(2)}, u32[]{:S(2)}) collective-permute-start(bf16[1,2,128,512]{3,2,1,0:T(8,128)(2,1)} %param.7), channel_id=1, source_target_pairs={{1,0},{2,1},{3,2},{4,3},{5,4},{6,5},{7,6},{8,7},{9,8},{10,9},{11,1... | collective-permute-start | bytes 786440 | tf_op jit(solution)/shard_map/ppermute | solution.py:15
  9.2 13.7 %collective-permute-start.5 = (bf16[1,2,128,512]{3,2,1,0:T(8,128)(2,1)}, bf16[1,2,128,512]{3,2,1,0:T(8,128)(2,1)S(1)}, u32[]{:S(2)}, u32[]{:S(2)}) collective-permute-start(bf16[1,2,128,512]{3,2,1,0:T(8,128)(2,1)} %param.7), channel_id=1, source_target_pairs={{2,0},{3,1},{4,2},{5,3},{6,4},{7,5},{8,6},{9,7},{10,8},{11,9},{12,... | collective-permute-start | bytes 786440 | tf_op jit(solution)/shard_map/ppermute | solution.py:15
  12.7 10.3 %copy-start.6 = (bf16[1,2,128,512]{3,2,1,0:T(8,128)(2,1)}, bf16[1,2,128,512]{3,2,1,0:T(8,128)(2,1)S(1)}, u32[]{:S(2)}) copy-start(bf16[1,2,128,512]{3,2,1,0:T(8,128)(2,1)S(1)} %collective-permute-done.4) | copy-start | bytes 786436
  22.9 0.7 copy-start.7
  23.6 2.9 %collective-permute-start.6 = (bf16[3,1,128,512]{3,2,1,0:T(8,128)(2,1)S(1)}, bf16[3,1,128,512]{3,2,1,0:T(8,128)(2,1)S(1)}, u32[]{:S(2)}, u32[]{:S(2)}) collective-permute-start(bf16[3,1,128,512]{3,2,1,0:T(8,128)(2,1)S(1)} %get-tuple-element.56), channel_id=1, source_target_pairs={} | collective-permute-start | bytes 1179656 | tf_op jit(solution)/shard_map/ppermute | solution.py:25
  24.3 2.3 %collective-permute-start.7 = (bf16[3,1,128,512]{3,2,1,0:T(8,128)(2,1)S(1)}, bf16[3,1,128,512]{3,2,1,0:T(8,128)(2,1)S(1)}, u32[]{:S(2)}, u32[]{:S(2)}) collective-permute-start(bf16[3,1,128,512]{3,2,1,0:T(8,128)(2,1)S(1)} %get-tuple-element.57), channel_id=1, source_target_pairs={} | collective-permute-start | bytes 1179656 | tf_op jit(solution)/shard_map/ppermute | solution.py:26
  117.7 17.6 %copy-start = (bf16[27,512,512]{2,1,0:T(8,128)(2,1)S(1)}, bf16[27,512,512]{2,1,0:T(8,128)(2,1)}, u32[]{:S(2)}) copy-start(bf16[27,512,512]{2,1,0:T(8,128)(2,1)} %all-gather.2.cloned.1.call-done) | copy-start | bytes 42467332
  117.7 18.9 %copy-start.5 = (bf16[1,2,128,512]{3,2,1,0:T(8,128)(2,1)S(1)}, bf16[1,2,128,512]{3,2,1,0:T(8,128)(2,1)}, u32[]{:S(2)}) copy-start(bf16[1,2,128,512]{3,2,1,0:T(8,128)(2,1)} %get-tuple-element.9) | copy-start | bytes 786436
  117.7 19.2 %copy-start.4 = (bf16[1,2,128,512]{3,2,1,0:T(8,128)(2,1)S(1)}, bf16[1,2,128,512]{3,2,1,0:T(8,128)(2,1)}, u32[]{:S(2)}) copy-start(bf16[1,2,128,512]{3,2,1,0:T(8,128)(2,1)} %get-tuple-element.10) | copy-start | bytes 786436
  117.7 19.6 %copy-start.3 = (bf16[1,2,128,512]{3,2,1,0:T(8,128)(2,1)S(1)}, bf16[1,2,128,512]{3,2,1,0:T(8,128)(2,1)}, u32[]{:S(2)}) copy-start(bf16[1,2,128,512]{3,2,1,0:T(8,128)(2,1)} %get-tuple-element.11) | copy-start | bytes 786436
  137.9 4.2 %copy-start.1 = (bf16[1,2,128,512]{3,2,1,0:T(8,128)(2,1)S(1)}, bf16[1,2,128,512]{3,2,1,0:T(8,128)(2,1)}, u32[]{:S(2)}) copy-start(bf16[1,2,128,512]{3,2,1,0:T(8,128)(2,1)} %param.4) | copy-start | bytes 786436
  137.9 4.2 %copy-start.8 = (f32[512]{0:T(512)S(1)}, f32[512]{0:T(512)}, u32[]{:S(2)}) copy-start(f32[512]{0:T(512)} %param.5) | copy-start | bytes 6148
  142.1 23.3 %slice-start = ((s8[14155776]{0:T(1024)(128)(4,1)}), s8[1572864]{0:T(1024)(128)(4,1)S(1)}, s32[]{:S(2)}) async-start(s8[14155776]{0:T(1024)(128)(4,1)} %bitcast.219), calls=%async_computation.1 | async-start | bytes 3145728
  142.5 7.8 %collective-permute-start.1 = (bf16[1,2,128,512]{3,2,1,0:T(8,128)(2,1)S(1)}, bf16[1,2,128,512]{3,2,1,0:T(8,128)(2,1)S(1)}, u32[]{:S(2)}, u32[]{:S(2)}) collective-permute-start(bf16[1,2,128,512]{3,2,1,0:T(8,128)(2,1)S(1)} %get-tuple-element.60), channel_id=1, source_target_pairs={{0,1},{1,2},{2,3},{3,4},{4,5},{5,6},{6,7},{7,8},{8,9},{9,10},{10,1... | collective-permute-start | bytes 786440 | tf_op jit(solution)/shard_map/ppermute | solution.py:15
  144.8 9.8 %collective-permute-start = (bf16[1,2,128,512]{3,2,1,0:T(8,128)(2,1)S(1)}, bf16[1,2,128,512]{3,2,1,0:T(8,128)(2,1)S(1)}, u32[]{:S(2)}, u32[]{:S(2)}) collective-permute-start(bf16[1,2,128,512]{3,2,1,0:T(8,128)(2,1)S(1)} %get-tuple-element.60), channel_id=1, source_target_pairs={{0,2},{1,3},{2,4},{3,5},{4,6},{5,7},{6,8},{7,9},{8,10},{9,11},{10,... | collective-permute-start | bytes 786440 | tf_op jit(solution)/shard_map/ppermute | solution.py:15
  154.8 4.4 %collective-permute-start.2 = (bf16[3,1,128,512]{3,2,1,0:T(8,128)(2,1)S(1)}, bf16[3,1,128,512]{3,2,1,0:T(8,128)(2,1)S(1)}, u32[]{:S(2)}, u32[]{:S(2)}) collective-permute-start(bf16[3,1,128,512]{3,2,1,0:T(8,128)(2,1)S(1)} %get-tuple-element.58), channel_id=1, source_target_pairs={} | collective-permute-start | bytes 1179656 | tf_op jit(solution)/shard_map/ppermute | solution.py:25
  155.5 3.7 %collective-permute-start.3 = (bf16[3,1,128,512]{3,2,1,0:T(8,128)(2,1)S(1)}, bf16[3,1,128,512]{3,2,1,0:T(8,128)(2,1)S(1)}, u32[]{:S(2)}, u32[]{:S(2)}) collective-permute-start(bf16[3,1,128,512]{3,2,1,0:T(8,128)(2,1)S(1)} %get-tuple-element.59), channel_id=1, source_target_pairs={} | collective-permute-start | bytes 1179656 | tf_op jit(solution)/shard_map/ppermute | solution.py:26
  156.3 9.1 %slice-start.1 = ((s8[14155776]{0:T(1024)(128)(4,1)}), s8[4194304]{0:T(1024)(128)(4,1)S(1)}, s32[]{:S(2)}) async-start(s8[14155776]{0:T(1024)(128)(4,1)} %bitcast.219), calls=%async_computation.2 | async-start | bytes 8388608
  160.0 5.5 %slice-start.2 = ((s8[14155776]{0:T(1024)(128)(4,1)}), s8[4194304]{0:T(1024)(128)(4,1)S(1)}, s32[]{:S(2)}) async-start(s8[14155776]{0:T(1024)(128)(4,1)} %bitcast.219), calls=%async_computation.3 | async-start | bytes 8388608
  160.7 4.7 %slice-start.3 = ((s8[14155776]{0:T(1024)(128)(4,1)}), s8[4194304]{0:T(1024)(128)(4,1)S(1)}, s32[]{:S(2)}) async-start(s8[14155776]{0:T(1024)(128)(4,1)} %bitcast.219), calls=%async_computation.4 | async-start | bytes 8388608
Sparse Core Ops, SparseCore 0:
  10.9 106.6 all-gather.1
where the time goes:
time: 182 us; the launch traced here: 181 us
  waiting for transfers between devices  103 us (57%)
  matrix products  39.8 us (22%)
  between operations  14.8 us (8%)
  starting transfers between devices  11.2 us (6%)
  other arithmetic  6.58 us (4%)
  local copies, waits for them, and re-layouts  5.17 us (3%)
    all_gather x1, waiting for transfers between devices, shards(): full_weight = lax.all_gather(conv_weight, 'tm', axis=1, tiled=True)  87.8 us
    dot_general x27, matrix products, shards(): lax.dot_general(back_window.reshape(-1, channels), tap_weight, (((1,), (1...  24.2 us
    dot_general x27, matrix products, shards(): jnp.dot(window.reshape(-1, channels), tap_weight, preferred_element_type=...  15.7 us
    ppermute x4, waiting for transfers between devices, shifted(): return lax.ppermute(block, axis, route)  14.5 us
    ppermute x4, starting transfers between devices, shifted(): return lax.ppermute(block, axis, route)  8.27 us
  transfers between devices with their start and end apart: 9, of which 3 were waited for; matrix products, arithmetic and copies ran while one was open for 7% of the time, Pallas kernels for 0%

commit v1 on v0

--- a/solution.py
+++ b/solution.py
@@ -1,6 +1,10 @@
+import functools
+
 import jax
 import jax.numpy as jnp
 from jax import lax
+from jax.experimental import pallas as pl
+from jax.experimental.pallas import tpu as pltpu
 from jax.sharding import PartitionSpec as P
 
 GROUPS = 32
@@ -38,7 +42,393 @@
     return jnp.pad(values, ((0, 0), (0, 0), (1, 1), (0, 0)))
 
 
+def group_mean(row, group, cells):
+    channels = row.shape[1]
+    shift = group.bit_length() - 1
+    shape = (channels, channels)
+    left = lax.shift_right_logical(lax.broadcasted_iota(jnp.int32, shape, 0), shift)
+    right = lax.shift_right_logical(lax.broadcasted_iota(jnp.int32, shape, 1), shift)
+    same = jnp.where(left == right, 1.0, 0.0).astype(jnp.float32)
+    wide = jnp.broadcast_to(row, (8, channels))
+    sums = jnp.dot(
+        wide, same, preferred_element_type=jnp.float32, precision=lax.Precision.HIGHEST
+    )
+    return sums[0:1] / cells
+
+
+def sums_of(values):
+    return jnp.sum(values, axis=0, keepdims=True)
+
+
+def block_kernel(
+    n,
+    columns,
+    latent_ref,
+    gain_ref,
+    weight_ref,
+    grad_ref,
+    refined_ref,
+    out_ref,
+    whole,
+    act_halo,
+    grad_halo,
+    act_wide,
+    grad_wide,
+    normed_ref,
+    inverse_ref,
+    conv_acc,
+    grad_acc,
+    own_sem,
+    send_sem,
+    recv_sem,
+    halo_send,
+    halo_recv,
+):
+    me = lax.axis_index("tm")
+    depth = n // 8
+    core = lax.rem(me, 2)
+    px = lax.rem(lax.div(me, 2), 2)
+    py = lax.rem(lax.div(me, 4), 2)
+    pz = lax.div(me, 8)
+    cells, channels = latent_ref.shape
+    taps = weight_ref.shape[0]
+    group = channels // GROUPS
+    neighbour = {
+        "x": me + 2 - 4 * px,
+        "y": me + 4 - 8 * py,
+        "core": me + 1 - 2 * core,
+        "up": me + 8,
+        "down": me - 8,
+    }
+
+    own_copy = pltpu.make_async_copy(weight_ref, whole.at[:, pz, py, px, core], own_sem)
+    own_copy.start()
+
+    barrier = pltpu.get_barrier_semaphore()
+
+    def greet(other):
+        pl.semaphore_signal(
+            barrier, inc=1, device_id={"tm": other}, device_id_type=pl.DeviceIdType.MESH
+        )
+
+    for name in ("x", "y", "core"):
+        greet(neighbour[name])
+    linked = [
+        (pz < depth - 1, me + 8),
+        (pz > 0, me - 8),
+        (me < n - 1, me + 1),
+        (me < n - 2, me + 2),
+        (me > 0, me - 1),
+        (me > 1, me - 2),
+    ]
+    expected = jnp.int32(3)
+    for there, other in linked:
+        pl.when(there)(functools.partial(greet, other))
+        expected = expected + there.astype(jnp.int32)
+    own_copy.wait()
+    pl.semaphore_wait(barrier, expected)
+
+    n_last_z = taps // 5
+    n_b = (taps - n_last_z) // 2
+    n_c = taps - n_last_z - n_b
+    rounds = n_c
+    kinds = [
+        (("z", "x", "y"), 0, n_b, 1),
+        (("z", "y", "x"), n_b, n_c, 1),
+        (("x", "y", "z"), n_b + n_c, n_last_z, 2),
+    ]
+    slots = {("up", s): s for s in range(depth - 1)}
+    slots.update({("down", s): depth - 1 + s for s in range(depth - 1)})
+    for name in ("x", "y", "core"):
+        slots[name] = len(slots)
+
+    def item(tap, held, **at):
+        parts = [
+            at.get(name, slice(None) if name in held else mine)
+            for name, mine in (("z", pz), ("y", py), ("x", px), ("core", core))
+        ]
+        return whole.at[(tap, *parts)]
+
+    def copy(kind, tap, what, target, slot):
+        return pltpu.make_async_remote_copy(
+            src_ref=what,
+            dst_ref=what,
+            send_sem=send_sem.at[kind, slots[slot]],
+            recv_sem=recv_sem.at[0 if isinstance(tap, pl.Slice) else tap, slots[slot]],
+            device_id={"tm": target},
+            device_id_type=pl.DeviceIdType.MESH,
+        )
+
+    def steps_of(kind, order):
+        sends, receives, waits = [], [], []
+        held = ()
+
+        def hop(name, held):
+            other = {"x": 1 - px, "y": 1 - py, "core": 1 - core}[name]
+            sends.append(
+                [(None, lambda tap: copy(kind, tap, item(tap, held), neighbour[name], name))]
+            )
+            receives.append(
+                [
+                    (
+                        None,
+                        lambda tap: copy(
+                            kind, tap, item(tap, held, **{name: other}), neighbour[name], name
+                        ),
+                    )
+                ]
+            )
+
+        def line(step, held):
+            def sent(way, sign):
+                return lambda tap: copy(
+                    kind, tap, item(tap, held, z=pz - sign * step), neighbour[way], (way, step)
+                )
+
+            def got(way, sign):
+                return lambda tap: copy(
+                    kind,
+                    tap,
+                    item(tap, held, z=pz - sign * (step + 1)),
+                    neighbour["down" if way == "up" else "up"],
+                    (way, step),
+                )
+
+            sends.append(
+                [
+                    ((pz < depth - 1) & (pz - step >= 0), sent("up", 1)),
+                    ((pz > 0) & (pz + step <= depth - 1), sent("down", -1)),
+                ]
+            )
+            receives.append(
+                [
+                    (pz - step - 1 >= 0, got("up", 1)),
+                    (pz + step + 1 <= depth - 1, got("down", -1)),
+                ]
+            )
+
+        for name in order + ("core",):
+            if name == "z":
+                for step in range(depth - 1):
+                    line(step, held)
+            else:
+                hop(name, held)
+            held = held + (name,)
+        return sends, receives
+
+    plans = [steps_of(kind, entry[0]) for kind, entry in enumerate(kinds)]
+    stages = len(plans[0][0])
+
+    def guarded(condition, action):
+        if condition is None:
+            action()
+        else:
+            pl.when(condition)(action)
+
+    def tap_of(kind, r):
+        order, first, count, every = kinds[kind]
+        if every == 1:
+            return first + r, (r >= 0) & (r < count)
+        return first + lax.div(r, every), (r >= 0) & (r < count * every) & (lax.rem(r, every) == 0)
+
+    def advance(tick, low, high):
+        for stage in range(high - 1, low - 1, -1):
+            for kind in range(len(kinds)):
+                tap, valid = tap_of(kind, tick - stage)
+                sends, receives = plans[kind]
+
+                @pl.when(valid)
+                def _():
+                    if stage > 0:
+                        for condition, make in receives[stage - 1]:
+                            guarded(condition, lambda: make(tap).wait_recv())
+                    if stage < stages:
+                        for condition, make in sends[stage]:
+                            guarded(condition, lambda: make(tap).start())
+
+    def use_tap(tap):
+        a = lax.div(tap, 9)
+        b = lax.rem(lax.div(tap, 3), 3)
+        e = lax.rem(tap, 3)
+        weights = whole[tap].reshape(channels, channels)
+        forward = act_wide[a, e, pl.ds(pl.multiple_of(b * columns, columns), cells)]
+        conv_acc[...] += jnp.dot(forward, weights, preferred_element_type=jnp.float32)
+        back = grad_wide[
+            2 - a, 2 - e, pl.ds(pl.multiple_of((2 - b) * columns, columns), cells)
+        ]
+        grad_acc[...] += lax.dot_general(
+            back, weights, (((1,), (1,)), ((), ())), preferred_element_type=jnp.float32
+        )
+
+    def compute(tick):
+        for kind in range(len(kinds)):
+            tap, valid = tap_of(kind, tick - stages)
+            pl.when(valid)(functools.partial(use_tap, tap))
+
+    def halo(source, target, place, slot):
+        return pltpu.make_async_remote_copy(
+            src_ref=source,
+            dst_ref=place,
+            send_sem=halo_send.at[slot],
+            recv_sem=halo_recv.at[slot],
+            device_id={"tm": target},
+            device_id_type=pl.DeviceIdType.MESH,
+        )
+
+    own_act = act_halo.at[2]
+    grad_copies = [
+        (me > d, me < n - 1 - d, halo(grad_ref, me - 1 - d, grad_halo.at[d], d)) for d in range(2)
+    ]
+    act_copies = [
+        (me < n - 1 - d, me > d, halo(own_act, me + 1 + d, act_halo.at[1 - d], 2 + d))
+        for d in range(2)
+    ]
+
+    advance(0, 0, 1)
+    for sends_it, _, this in grad_copies:
+        pl.when(sends_it)(this.start)
+
+    latent_wide = latent_ref[...].astype(jnp.float32)
+    gain = gain_ref[...]
+    count = cells * group
+    average = group_mean(sums_of(latent_wide), group, count)
+    centred = latent_wide - average
+    spread = group_mean(sums_of(centred * centred), group, count)
+    inverse = lax.rsqrt(spread + epsilon)
+    inverse_ref[...] = inverse
+    normed = centred * inverse
+    normed_ref[...] = normed
+    scaled = normed * gain
+    activated = scaled * jax.nn.sigmoid(scaled)
+    own_act[...] = activated.astype(jnp.bfloat16)
+    for sends_it, _, this in act_copies:
+        pl.when(sends_it)(this.start)
+    conv_acc[...] = jnp.zeros_like(conv_acc)
+    grad_acc[...] = jnp.zeros_like(grad_acc)
+
+    def early(tick, carry):
+        advance(tick, 0, stages)
+        return carry
+
+    lax.fori_loop(1, stages - 1, early, 0)
+
+    column = lax.rem(lax.broadcasted_iota(jnp.int32, (cells, channels), 0), columns)
+    edge = jnp.zeros((columns, channels), jnp.bfloat16)
+
+    def widen(frame, wide, place):
+        values = frame.astype(jnp.float32)
+        left = jnp.where(column == 0, 0.0, pltpu.roll(values, 1, 0))
+        right = jnp.where(column == columns - 1, 0.0, pltpu.roll(values, cells - 1, 0))
+        for e, part in enumerate((left, values, right)):
+            wide[place, e, 0:columns] = edge
+            wide[place, e, columns : columns + cells] = part.astype(jnp.bfloat16)
+            wide[place, e, columns + cells : 2 * columns + cells] = edge
+
+    widen(act_halo[2], act_wide, 2)
+    widen(grad_ref[...], grad_wide, 0)
+    for d in range(2):
+        for copies, buffer, wide, place, at in (
+            (grad_copies, grad_halo, grad_wide, d + 1, d),
+            (act_copies, act_halo, act_wide, 1 - d, 1 - d),
+        ):
+            _, gets_it, this = copies[d]
+            pl.when(gets_it)(this.wait_recv)
+
+            @pl.when(jnp.logical_not(gets_it))
+            def _():
+                buffer[at] = jnp.zeros((cells, channels), jnp.bfloat16)
+
+            widen(buffer[at], wide, place)
+
+    def late(tick, carry):
+        advance(tick, 0, stages + 1)
+        compute(tick)
+        return carry
+
+    lax.fori_loop(stages - 1, rounds + stages, late, 0)
+
+    refined_ref[...] = (latent_ref[...].astype(jnp.float32) + conv_acc[...]).astype(jnp.bfloat16)
+    normed = normed_ref[...]
+    scaled = normed * gain
+    s = jax.nn.sigmoid(scaled)
+    grad_normed = grad_acc[...] * s * (1.0 + scaled * (1.0 - s)) * gain
+    first = group_mean(sums_of(grad_normed), group, count)
+    second = group_mean(sums_of(grad_normed * normed), group, count)
+    out_ref[...] = grad_ref[...].astype(jnp.float32) + (
+        grad_normed - first - normed * second
+    ) * inverse_ref[...]
+
+    for sends_it, _, this in grad_copies + act_copies:
+        pl.when(sends_it)(this.wait_send)
+    for kind, (order, first_tap, count_taps, _) in enumerate(kinds):
+        for stage in plans[kind][0]:
+            for condition, make in stage:
+                guarded(
+                    condition,
+                    lambda: make(pl.ds(first_tap, count_taps)).wait_send(),
+                )
+
+
+def fused(latent, norm_gain, conv_weight, grad_out):
+    n = lax.axis_size("tm")
+    _, rows_here, columns, channels = latent.shape
+    cells = rows_here * columns
+    taps, depth = conv_weight.shape[:2]
+    line = n // 8
+    slots = 2 * (line - 1) + 3
+    bf16, f32 = jnp.bfloat16, jnp.float32
+    wide = (3, 3, cells + 2 * columns, channels)
+    vmem = pl.BlockSpec(memory_space=pltpu.VMEM)
+    refined, grad_latent = pl.pallas_call(
+        functools.partial(block_kernel, n, columns),
+        out_shape=(
+            jax.ShapeDtypeStruct((cells, channels), bf16),
+            jax.ShapeDtypeStruct((cells, channels), f32),
+        ),
+        in_specs=[vmem, vmem, pl.BlockSpec(memory_space=pl.ANY), vmem],
+        out_specs=(vmem, vmem),
+        scratch_shapes=[
+            pltpu.VMEM((taps, line, 2, 2, 2, depth, channels), bf16),
+            pltpu.VMEM((3, cells, channels), bf16),
+            pltpu.VMEM((2, cells, channels), bf16),
+            pltpu.VMEM(wide, bf16),
+            pltpu.VMEM(wide, bf16),
+            pltpu.VMEM((cells, channels), f32),
+            pltpu.VMEM((1, channels), f32),
+            pltpu.VMEM((cells, channels), f32),
+            pltpu.VMEM((cells, channels), f32),
+            pltpu.SemaphoreType.DMA,
+            pltpu.SemaphoreType.DMA((3, slots)),
+            pltpu.SemaphoreType.DMA((taps, slots)),
+            pltpu.SemaphoreType.DMA((4,)),
+            pltpu.SemaphoreType.DMA((4,)),
+        ],
+        compiler_params=pltpu.CompilerParams(
+            collective_id=0, has_side_effects=True, vmem_limit_bytes=52 * 2**20
+        ),
+        cost_estimate=pl.CostEstimate(
+            flops=4 * taps * cells * channels * channels,
+            bytes_accessed=taps * channels * channels * 2,
+            transcendentals=2 * cells * channels,
+        ),
+    )(
+        latent.reshape(cells, channels),
+        norm_gain.reshape(1, channels),
+        conv_weight,
+        grad_out.reshape(cells, channels),
+    )
+    return refined.reshape(latent.shape), grad_latent.reshape(latent.shape)
+
+
 def shards(latent, norm_gain, conv_weight, grad_out):
+    group = latent.shape[3] // GROUPS
+    whole_frame = lax.axis_size("rows") == 1 and latent.shape[0] == 1
+    if whole_frame and lax.axis_size("tm") % 8 == 0 and group & (group - 1) == 0:
+        return fused(latent, norm_gain, conv_weight, grad_out)
+    return general(latent, norm_gain, conv_weight, grad_out)
+
+
+def general(latent, norm_gain, conv_weight, grad_out):
     frames_here, rows_here, columns, channels = latent.shape
     cell_count = lax.axis_size("rows") * rows_here * columns * (channels // GROUPS)
     full_weight = lax.all_gather(conv_weight, "tm", axis=1, tiled=True)

time: 182 us -> 104 us (0.57)
  the two profiles are of different devices: /device:TPU:0 before, /device:TPU:27 now
where the time goes in v1:
time: 104 us; the launch traced here: 103 us
  Pallas kernels  97.8 us (94%)
  local copies, waits for them, and re-layouts  5.08 us (5%)
    pallas_call x1, Pallas kernels, fused(): pl.pallas_call(functools.partial(block_kernel, n, columns), out_shape=(ja...  97.8 us
    unnamed x10, local copies, waits for them, and re-layouts  5.08 us

profile of v1, /device:TPU:27, one launch (start us, length us, event | category | flops | bytes accessed | tf_op | source)
XLA Modules:
  0.0 103.5 jit_solution(5327187102344981837)
XLA Ops:
  0.6 0.0 copy-start.3
  0.6 0.7 copy-done.3
  1.3 0.0 copy-start
  1.3 1.0 copy-done
  2.3 0.0 copy-start.1
  2.3 0.9 copy-done.1
  3.3 0.0 copy-start.2
  3.3 0.9 copy-done.2
  4.2 97.8 %shard_map.59 = (bf16[256,512]{1,0:T(8,128)(2,1)S(1)}, f32[256,512]{1,0:T(8,128)S(1)}) custom-call(bf16[256,512]{1,0:T(8,128)(2,1)S(1)} %bitcast.7, f32[1,512]{1,0:T(1,128)S(1)} %bitcast.9, bf16[27,16,512]{2,1,0:T(8,128)(2,1)S(1)} %copy-done, bf16[256,512]{1,0:T(8,128)(2,1)S(1)} %bitcast.8), custom_call_target="tpu_custom_call" | custom-call | flops 7247757312 | bytes 14155776 | tf_op jit(solution)/shard_map/pallas_call | solution.py:382
  102.0 0.7 copy.8
  102.7 0.8 copy.9
Async XLA Ops:
  0.6 0.7 copy-start.3
  1.3 1.0 copy-start
  2.3 0.9 copy-start.1
  3.3 0.9 copy-start.2

commit v2 on v1

--- a/solution.py
+++ b/solution.py
@@ -63,12 +63,15 @@
 def block_kernel(
     n,
     columns,
+    latent_hbm,
+    gain_hbm,
+    weight_ref,
+    grad_hbm,
+    refined_ref,
+    out_ref,
     latent_ref,
     gain_ref,
-    weight_ref,
     grad_ref,
-    refined_ref,
-    out_ref,
     whole,
     act_halo,
     grad_halo,
@@ -79,6 +82,7 @@
     conv_acc,
     grad_acc,
     own_sem,
+    fetch_sem,
     send_sem,
     recv_sem,
     halo_send,
@@ -103,6 +107,14 @@
 
     own_copy = pltpu.make_async_copy(weight_ref, whole.at[:, pz, py, px, core], own_sem)
     own_copy.start()
+    fetches = [
+        pltpu.make_async_copy(source, place, fetch_sem.at[i])
+        for i, (source, place) in enumerate(
+            ((grad_hbm, grad_ref), (latent_hbm, latent_ref), (gain_hbm, gain_ref))
+        )
+    ]
+    for fetch in fetches:
+        fetch.start()
 
     barrier = pltpu.get_barrier_semaphore()
 
@@ -128,10 +140,11 @@
     own_copy.wait()
     pl.semaphore_wait(barrier, expected)
 
-    n_last_z = taps // 5
+    n_last_z = (2 * taps) // 9
     n_b = (taps - n_last_z) // 2
     n_c = taps - n_last_z - n_b
     rounds = n_c
+    lag = 2
     kinds = [
         (("z", "x", "y"), 0, n_b, 1),
         (("z", "y", "x"), n_b, n_c, 1),
@@ -234,7 +247,7 @@
     def advance(tick, low, high):
         for stage in range(high - 1, low - 1, -1):
             for kind in range(len(kinds)):
-                tap, valid = tap_of(kind, tick - stage)
+                tap, valid = tap_of(kind, tick - lag * stage)
                 sends, receives = plans[kind]
 
                 @pl.when(valid)
@@ -262,7 +275,7 @@
 
     def compute(tick):
         for kind in range(len(kinds)):
-            tap, valid = tap_of(kind, tick - stages)
+            tap, valid = tap_of(kind, tick - lag * stages)
             pl.when(valid)(functools.partial(use_tap, tap))
 
     def halo(source, target, place, slot):
@@ -284,7 +297,10 @@
         for d in range(2)
     ]
 
-    advance(0, 0, 1)
+    for tick in range(lag):
+        advance(tick, 0, 1)
+    for fetch in fetches:
+        fetch.wait()
     for sends_it, _, this in grad_copies:
         pl.when(sends_it)(this.start)
 
@@ -306,12 +322,6 @@
     conv_acc[...] = jnp.zeros_like(conv_acc)
     grad_acc[...] = jnp.zeros_like(grad_acc)
 
-    def early(tick, carry):
-        advance(tick, 0, stages)
-        return carry
-
-    lax.fori_loop(1, stages - 1, early, 0)
-
     column = lax.rem(lax.broadcasted_iota(jnp.int32, (cells, channels), 0), columns)
     edge = jnp.zeros((columns, channels), jnp.bfloat16)
 
@@ -324,28 +334,39 @@
             wide[place, e, columns : columns + cells] = part.astype(jnp.bfloat16)
             wide[place, e, columns + cells : 2 * columns + cells] = edge
 
-    widen(act_halo[2], act_wide, 2)
-    widen(grad_ref[...], grad_wide, 0)
-    for d in range(2):
-        for copies, buffer, wide, place, at in (
-            (grad_copies, grad_halo, grad_wide, d + 1, d),
-            (act_copies, act_halo, act_wide, 1 - d, 1 - d),
-        ):
-            _, gets_it, this = copies[d]
-            pl.when(gets_it)(this.wait_recv)
-
-            @pl.when(jnp.logical_not(gets_it))
-            def _():
-                buffer[at] = jnp.zeros((cells, channels), jnp.bfloat16)
-
-            widen(buffer[at], wide, place)
+    def take(copies, d, buffer, at, wide, place):
+        _, gets_it, this = copies[d]
+        pl.when(gets_it)(this.wait_recv)
+
+        @pl.when(jnp.logical_not(gets_it))
+        def _():
+            buffer[at] = jnp.zeros((cells, channels), jnp.bfloat16)
+
+        widen(buffer[at], wide, place)
+
+    jobs = [
+        lambda: widen(act_halo[2], act_wide, 2),
+        lambda: widen(grad_ref[...], grad_wide, 0),
+        lambda: take(grad_copies, 0, grad_halo, 0, grad_wide, 1),
+        lambda: take(act_copies, 0, act_halo, 1, act_wide, 1),
+        lambda: take(grad_copies, 1, grad_halo, 1, grad_wide, 2),
+        lambda: take(act_copies, 1, act_halo, 0, act_wide, 0),
+    ]
+
+    def early(tick, carry):
+        advance(tick, 0, stages)
+        for i, job in enumerate(jobs):
+            pl.when(tick == lag + 1 + i)(job)
+        return carry
+
+    lax.fori_loop(lag, lag * stages - 1, early, 0)
 
     def late(tick, carry):
         advance(tick, 0, stages + 1)
         compute(tick)
         return carry
 
-    lax.fori_loop(stages - 1, rounds + stages, late, 0)
+    lax.fori_loop(lag * stages - 1, rounds + lag * stages, late, 0)
 
     refined_ref[...] = (latent_ref[...].astype(jnp.float32) + conv_acc[...]).astype(jnp.bfloat16)
     normed = normed_ref[...]
@@ -379,15 +400,19 @@
     bf16, f32 = jnp.bfloat16, jnp.float32
     wide = (3, 3, cells + 2 * columns, channels)
     vmem = pl.BlockSpec(memory_space=pltpu.VMEM)
+    far = pl.BlockSpec(memory_space=pltpu.HBM)
     refined, grad_latent = pl.pallas_call(
         functools.partial(block_kernel, n, columns),
         out_shape=(
             jax.ShapeDtypeStruct((cells, channels), bf16),
             jax.ShapeDtypeStruct((cells, channels), f32),
         ),
-        in_specs=[vmem, vmem, pl.BlockSpec(memory_space=pl.ANY), vmem],
+        in_specs=[far] * 4,
         out_specs=(vmem, vmem),
         scratch_shapes=[
+            pltpu.VMEM((cells, channels), bf16),
+            pltpu.VMEM((1, channels), f32),
+            pltpu.VMEM((cells, channels), bf16),
             pltpu.VMEM((taps, line, 2, 2, 2, depth, channels), bf16),
             pltpu.VMEM((3, cells, channels), bf16),
             pltpu.VMEM((2, cells, channels), bf16),
@@ -398,13 +423,14 @@
             pltpu.VMEM((cells, channels), f32),
             pltpu.VMEM((cells, channels), f32),
             pltpu.SemaphoreType.DMA,
+            pltpu.SemaphoreType.DMA((3,)),
             pltpu.SemaphoreType.DMA((3, slots)),
             pltpu.SemaphoreType.DMA((taps, slots)),
             pltpu.SemaphoreType.DMA((4,)),
             pltpu.SemaphoreType.DMA((4,)),
         ],
         compiler_params=pltpu.CompilerParams(
-            collective_id=0, has_side_effects=True, vmem_limit_bytes=52 * 2**20
+            collective_id=0, has_side_effects=True, vmem_limit_bytes=64 * 2**20 - 2**17
         ),
         cost_estimate=pl.CostEstimate(
             flops=4 * taps * cells * channels * channels,

time: 104 us -> 86.7 us (0.83)
  the two profiles are of different devices: /device:TPU:27 before, /device:TPU:0 now
where the time goes in v2:
time: 86.7 us; the launch traced here: 86.5 us
  Pallas kernels  83.3 us (96%)
  local copies, waits for them, and re-layouts  2.52 us (3%)
    pallas_call x1, Pallas kernels, fused(): pl.pallas_call(functools.partial(block_kernel, n, columns), out_shape=(ja...  83.3 us
    unnamed x4, local copies, waits for them, and re-layouts  2.52 us

profile of v2, /device:TPU:0, one launch (start us, length us, event | category | flops | bytes accessed | tf_op | source)
XLA Modules:
  0.0 86.5 jit_solution(10890562178669200392)
XLA Ops:
  0.6 83.3 %shard_map.59 = (bf16[256,512]{1,0:T(8,128)(2,1)}, f32[256,512]{1,0:T(8,128)}) custom-call(bf16[256,512]{1,0:T(8,128)(2,1)} %bitcast.7, f32[1,512]{1,0:T(1,128)} %bitcast.9, bf16[27,16,512]{2,1,0:T(8,128)(2,1)} %weight_ref.1, bf16[256,512]{1,0:T(8,128)(2,1)} %bitcast.8), custom_call_target="tpu_custom_call" | custom-call | flops 7247757312 | bytes 14155776 | tf_op jit(solution)/shard_map/pallas_call | solution.py:404
  84.0 0.0 copy-start
  84.0 1.7 %copy.8 = bf16[1,2,128,512]{3,2,1,0:T(8,128)(2,1)} copy(bf16[1,2,128,512]{3,2,1,0:T(8,128)(2,1)} %bitcast.6) | data formatting | bytes 524288
  85.7 0.0 copy-done
  85.7 0.8 copy.9
Async XLA Ops:
  84.0 1.7 %copy-start = (f32[256,512]{1,0:T(8,128)S(1)}, f32[256,512]{1,0:T(8,128)}, u32[]{:S(2)}) copy-start(f32[256,512]{1,0:T(8,128)} %get-tuple-element.5) | copy-start | bytes 1572868

commit v3 on v2

--- a/solution.py
+++ b/solution.py
@@ -140,15 +140,16 @@
     own_copy.wait()
     pl.semaphore_wait(barrier, expected)
 
-    n_last_z = (2 * taps) // 9
+    n_last_z = (taps + 1) // 4
     n_b = (taps - n_last_z) // 2
     n_c = taps - n_last_z - n_b
     rounds = n_c
-    lag = 2
+    line_first = (*range(depth), depth + 1, depth + 3, depth + 4)
+    line_last = (0, 1, *range(2, 2 * depth + 1, 2), 2 * depth + 1)
     kinds = [
-        (("z", "x", "y"), 0, n_b, 1),
-        (("z", "y", "x"), n_b, n_c, 1),
-        (("x", "y", "z"), n_b + n_c, n_last_z, 2),
+        (("z", "x", "y"), 0, n_b, line_first),
+        (("z", "y", "x"), n_b, n_c, line_first),
+        (("x", "y", "z"), n_b + n_c, n_last_z, line_last),
     ]
     slots = {("up", s): s for s in range(depth - 1)}
     slots.update({("down", s): depth - 1 + s for s in range(depth - 1)})
@@ -239,15 +240,19 @@
             pl.when(condition)(action)
 
     def tap_of(kind, r):
-        order, first, count, every = kinds[kind]
-        if every == 1:
+        _, first, count, _ = kinds[kind]
+        if count >= rounds - 1:
             return first + r, (r >= 0) & (r < count)
-        return first + lax.div(r, every), (r >= 0) & (r < count * every) & (lax.rem(r, every) == 0)
+        spread_out = r * count
+        return (
+            first + lax.div(spread_out, rounds),
+            (r >= 0) & (r < rounds) & (lax.rem(spread_out, rounds) < count),
+        )
 
     def advance(tick, low, high):
         for stage in range(high - 1, low - 1, -1):
             for kind in range(len(kinds)):
-                tap, valid = tap_of(kind, tick - lag * stage)
+                tap, valid = tap_of(kind, tick - kinds[kind][3][stage])
                 sends, receives = plans[kind]
 
                 @pl.when(valid)
@@ -275,14 +280,14 @@
 
     def compute(tick):
         for kind in range(len(kinds)):
-            tap, valid = tap_of(kind, tick - lag * stages)
+            tap, valid = tap_of(kind, tick - kinds[kind][3][stages])
             pl.when(valid)(functools.partial(use_tap, tap))
 
-    def halo(source, target, place, slot):
+    def halo(source, target, place, slot, again=0):
         return pltpu.make_async_remote_copy(
             src_ref=source,
             dst_ref=place,
-            send_sem=halo_send.at[slot],
+            send_sem=halo_send.at[slot + again],
             recv_sem=halo_recv.at[slot],
             device_id={"tm": target},
             device_id_type=pl.DeviceIdType.MESH,
@@ -290,15 +295,19 @@
 
     own_act = act_halo.at[2]
     grad_copies = [
-        (me > d, me < n - 1 - d, halo(grad_ref, me - 1 - d, grad_halo.at[d], d)) for d in range(2)
+        (me > 0, me < n - 1, halo(grad_ref, me - 1, grad_halo.at[0], 0)),
+        ((me > 1) & (core == 1), me < n - 2, halo(grad_ref, me - 2, grad_halo.at[1], 1)),
     ]
     act_copies = [
-        (me < n - 1 - d, me > d, halo(own_act, me + 1 + d, act_halo.at[1 - d], 2 + d))
-        for d in range(2)
-    ]
-
-    for tick in range(lag):
-        advance(tick, 0, 1)
+        (me < n - 1, me > 0, halo(own_act, me + 1, act_halo.at[1], 2)),
+        ((me < n - 2) & (core == 0), me > 1, halo(own_act, me + 2, act_halo.at[0], 3)),
+    ]
+    passed_on = [
+        ((me < n - 2) & (core == 1), halo(grad_halo.at[0], me - 1, grad_halo.at[1], 1, 4)),
+        ((me > 1) & (core == 0), halo(act_halo.at[1], me + 1, act_halo.at[0], 3, 4)),
+    ]
+
+    advance(0, 0, 1)
     for fetch in fetches:
         fetch.wait()
     for sends_it, _, this in grad_copies:
@@ -337,6 +346,9 @@
     def take(copies, d, buffer, at, wide, place):
         _, gets_it, this = copies[d]
         pl.when(gets_it)(this.wait_recv)
+        if d == 0:
+            passes, onward = passed_on[copies is act_copies]
+            pl.when(passes)(onward.start)
 
         @pl.when(jnp.logical_not(gets_it))
         def _():
@@ -356,17 +368,19 @@
     def early(tick, carry):
         advance(tick, 0, stages)
         for i, job in enumerate(jobs):
-            pl.when(tick == lag + 1 + i)(job)
+            pl.when(tick == 1 + i)(job)
         return carry
 
-    lax.fori_loop(lag, lag * stages - 1, early, 0)
+    first_use = min(entry[3][stages] for entry in kinds)
+    last_use = max(entry[3][stages] for entry in kinds)
+    lax.fori_loop(1, first_use, early, 0)
 
     def late(tick, carry):
         advance(tick, 0, stages + 1)
         compute(tick)
         return carry
 
-    lax.fori_loop(lag * stages - 1, rounds + lag * stages, late, 0)
+    lax.fori_loop(first_use, rounds + last_use, late, 0)
 
     refined_ref[...] = (latent_ref[...].astype(jnp.float32) + conv_acc[...]).astype(jnp.bfloat16)
     normed = normed_ref[...]
@@ -381,6 +395,8 @@
 
     for sends_it, _, this in grad_copies + act_copies:
         pl.when(sends_it)(this.wait_send)
+    for passes, onward in passed_on:
+        pl.when(passes)(onward.wait_send)
     for kind, (order, first_tap, count_taps, _) in enumerate(kinds):
         for stage in plans[kind][0]:
             for condition, make in stage:
@@ -426,7 +442,7 @@
             pltpu.SemaphoreType.DMA((3,)),
             pltpu.SemaphoreType.DMA((3, slots)),
             pltpu.SemaphoreType.DMA((taps, slots)),
-            pltpu.SemaphoreType.DMA((4,)),
+            pltpu.SemaphoreType.DMA((8,)),
             pltpu.SemaphoreType.DMA((4,)),
         ],
         compiler_params=pltpu.CompilerParams(

time: 86.7 us -> 78.6 us (0.907)
  Pallas kernels: 83.3 us -> 75.3 us
    pallas_call x1, Pallas kernels: 83.3 us -> 75.3 us  [fused(): pl.pallas_call(functools.partial(block_kernel, n, columns), out_shape=(ja...]
where the time goes in v3:
time: 78.6 us; the launch traced here: 78.5 us
  Pallas kernels  75.3 us (96%)
  local copies, waits for them, and re-layouts  2.52 us (3%)
    pallas_call x1, Pallas kernels, fused(): pl.pallas_call(functools.partial(block_kernel, n, columns), out_shape=(ja...  75.3 us
    unnamed x4, local copies, waits for them, and re-layouts  2.52 us

profile of v3, /device:TPU:0, one launch (start us, length us, event | category | flops | bytes accessed | tf_op | source)
XLA Modules:
  0.0 78.5 jit_solution(6632246276960272307)
XLA Ops:
  0.6 75.3 %shard_map.59 = (bf16[256,512]{1,0:T(8,128)(2,1)}, f32[256,512]{1,0:T(8,128)}) custom-call(bf16[256,512]{1,0:T(8,128)(2,1)} %bitcast.7, f32[1,512]{1,0:T(1,128)} %bitcast.9, bf16[27,16,512]{2,1,0:T(8,128)(2,1)} %weight_ref.1, bf16[256,512]{1,0:T(8,128)(2,1)} %bitcast.8), custom_call_target="tpu_custom_call" | custom-call | flops 7247757312 | bytes 14155776 | tf_op jit(solution)/shard_map/pallas_call | solution.py:420
  75.9 0.0 copy-start
  75.9 1.7 %copy.8 = bf16[1,2,128,512]{3,2,1,0:T(8,128)(2,1)} copy(bf16[1,2,128,512]{3,2,1,0:T(8,128)(2,1)} %bitcast.6) | data formatting | bytes 524288
  77.7 0.0 copy-done
  77.7 0.8 %copy.9 = f32[1,2,128,512]{3,2,1,0:T(8,128)} copy(f32[1,2,128,512]{3,2,1,0:T(8,128)S(1)} %bitcast.5) | data formatting | bytes 1048576
Async XLA Ops:
  75.9 1.7 %copy-start = (f32[256,512]{1,0:T(8,128)S(1)}, f32[256,512]{1,0:T(8,128)}, u32[]{:S(2)}) copy-start(f32[256,512]{1,0:T(8,128)} %get-tuple-element.5) | copy-start | bytes 1572868

commit v4 on v3

--- a/solution.py
+++ b/solution.py
@@ -42,18 +42,28 @@
     return jnp.pad(values, ((0, 0), (0, 0), (1, 1), (0, 0)))
 
 
-def group_mean(row, group, cells):
-    channels = row.shape[1]
+def fill_same(same_ref, group):
     shift = group.bit_length() - 1
-    shape = (channels, channels)
+    shape = same_ref.shape
     left = lax.shift_right_logical(lax.broadcasted_iota(jnp.int32, shape, 0), shift)
     right = lax.shift_right_logical(lax.broadcasted_iota(jnp.int32, shape, 1), shift)
-    same = jnp.where(left == right, 1.0, 0.0).astype(jnp.float32)
-    wide = jnp.broadcast_to(row, (8, channels))
-    sums = jnp.dot(
-        wide, same, preferred_element_type=jnp.float32, precision=lax.Precision.HIGHEST
-    )
-    return sums[0:1] / cells
+    same_ref[...] = jnp.where(left == right, 1.0, 0.0).astype(jnp.float32)
+
+
+def group_mean(rows, same_ref, cells):
+    return (
+        jnp.dot(
+            rows,
+            same_ref[...],
+            preferred_element_type=jnp.float32,
+            precision=lax.Precision.HIGHEST,
+        )
+        / cells
+    )
+
+
+def eight(row):
+    return jnp.broadcast_to(row, (8, row.shape[1]))
 
 
 def sums_of(values):
@@ -78,6 +88,8 @@
     act_wide,
     grad_wide,
     normed_ref,
+    slope_ref,
+    same_ref,
     inverse_ref,
     conv_acc,
     grad_acc,
@@ -137,6 +149,9 @@
     for there, other in linked:
         pl.when(there)(functools.partial(greet, other))
         expected = expected + there.astype(jnp.int32)
+    fill_same(same_ref, group)
+    conv_acc[...] = jnp.zeros_like(conv_acc)
+    grad_acc[...] = jnp.zeros_like(grad_acc)
     own_copy.wait()
     pl.semaphore_wait(barrier, expected)
 
@@ -268,15 +283,25 @@
         a = lax.div(tap, 9)
         b = lax.rem(lax.div(tap, 3), 3)
         e = lax.rem(tap, 3)
-        weights = whole[tap].reshape(channels, channels)
-        forward = act_wide[a, e, pl.ds(pl.multiple_of(b * columns, columns), cells)]
-        conv_acc[...] += jnp.dot(forward, weights, preferred_element_type=jnp.float32)
-        back = grad_wide[
-            2 - a, 2 - e, pl.ds(pl.multiple_of((2 - b) * columns, columns), cells)
-        ]
-        grad_acc[...] += lax.dot_general(
-            back, weights, (((1,), (1,)), ((), ())), preferred_element_type=jnp.float32
-        )
+        inner = cells - columns
+
+        def rows_of(out_first, in_first, count):
+            weights = whole[tap].reshape(channels, channels)
+            conv_acc[out_first : out_first + count] += jnp.dot(
+                act_wide[a, e, columns + in_first : columns + in_first + count],
+                weights,
+                preferred_element_type=jnp.float32,
+            )
+            grad_acc[in_first : in_first + count] += lax.dot_general(
+                grad_wide[2 - a, 2 - e, columns + out_first : columns + out_first + count],
+                weights,
+                (((1,), (1,)), ((), ())),
+                preferred_element_type=jnp.float32,
+            )
+
+        pl.when(b == 0)(lambda: rows_of(columns, 0, inner))
+        pl.when(b == 1)(lambda: rows_of(0, 0, cells))
+        pl.when(b == 2)(lambda: rows_of(0, columns, inner))
 
     def compute(tick):
         for kind in range(len(kinds)):
@@ -316,21 +341,19 @@
     latent_wide = latent_ref[...].astype(jnp.float32)
     gain = gain_ref[...]
     count = cells * group
-    average = group_mean(sums_of(latent_wide), group, count)
+    average = group_mean(eight(sums_of(latent_wide)), same_ref, count)[0:1]
     centred = latent_wide - average
-    spread = group_mean(sums_of(centred * centred), group, count)
+    spread = group_mean(eight(sums_of(centred * centred)), same_ref, count)[0:1]
     inverse = lax.rsqrt(spread + epsilon)
     inverse_ref[...] = inverse
     normed = centred * inverse
     normed_ref[...] = normed
     scaled = normed * gain
-    activated = scaled * jax.nn.sigmoid(scaled)
+    sigmoid_value = jax.nn.sigmoid(scaled)
+    activated = scaled * sigmoid_value
     own_act[...] = activated.astype(jnp.bfloat16)
     for sends_it, _, this in act_copies:
         pl.when(sends_it)(this.start)
-    conv_acc[...] = jnp.zeros_like(conv_acc)
-    grad_acc[...] = jnp.zeros_like(grad_acc)
-
     column = lax.rem(lax.broadcasted_iota(jnp.int32, (cells, channels), 0), columns)
     edge = jnp.zeros((columns, channels), jnp.bfloat16)
 
@@ -343,6 +366,13 @@
             wide[place, e, columns : columns + cells] = part.astype(jnp.bfloat16)
             wide[place, e, columns + cells : 2 * columns + cells] = edge
 
+    def keep_slope():
+        scaled = normed_ref[...] * gain_ref[...]
+        sigmoid_value = jax.nn.sigmoid(scaled)
+        slope_ref[...] = (
+            sigmoid_value * (1.0 + scaled * (1.0 - sigmoid_value)) * gain_ref[...]
+        )
+
     def take(copies, d, buffer, at, wide, place):
         _, gets_it, this = copies[d]
         pl.when(gets_it)(this.wait_recv)
@@ -357,6 +387,7 @@
         widen(buffer[at], wide, place)
 
     jobs = [
+        keep_slope,
         lambda: widen(act_halo[2], act_wide, 2),
         lambda: widen(grad_ref[...], grad_wide, 0),
         lambda: take(grad_copies, 0, grad_halo, 0, grad_wide, 1),
@@ -384,11 +415,14 @@
 
     refined_ref[...] = (latent_ref[...].astype(jnp.float32) + conv_acc[...]).astype(jnp.bfloat16)
     normed = normed_ref[...]
-    scaled = normed * gain
-    s = jax.nn.sigmoid(scaled)
-    grad_normed = grad_acc[...] * s * (1.0 + scaled * (1.0 - s)) * gain
-    first = group_mean(sums_of(grad_normed), group, count)
-    second = group_mean(sums_of(grad_normed * normed), group, count)
+    grad_normed = grad_acc[...] * slope_ref[...]
+    upper = lax.broadcasted_iota(jnp.int32, (8, channels), 0) < 4
+    means = group_mean(
+        jnp.where(upper, eight(sums_of(grad_normed)), eight(sums_of(grad_normed * normed))),
+        same_ref,
+        count,
+    )
+    first, second = means[0:1], means[4:5]
     out_ref[...] = grad_ref[...].astype(jnp.float32) + (
         grad_normed - first - normed * second
     ) * inverse_ref[...]
@@ -435,6 +469,8 @@
             pltpu.VMEM(wide, bf16),
             pltpu.VMEM(wide, bf16),
             pltpu.VMEM((cells, channels), f32),
+            pltpu.VMEM((cells, channels), f32),
+            pltpu.VMEM((channels, channels), f32),
             pltpu.VMEM((1, channels), f32),
             pltpu.VMEM((cells, channels), f32),
             pltpu.VMEM((cells, channels), f32),

time: 78.6 us -> 79 us (level)
  no operation moved by 1% of the time
where the time goes in v4:
time: 79 us; the launch traced here: 78.8 us
  Pallas kernels  75.6 us (96%)
  local copies, waits for them, and re-layouts  2.52 us (3%)
    pallas_call x1, Pallas kernels, fused(): pl.pallas_call(functools.partial(block_kernel, n, columns), out_shape=(ja...  75.6 us
    unnamed x4, local copies, waits for them, and re-layouts  2.52 us

profile of v4, /device:TPU:0, one launch (start us, length us, event | category | flops | bytes accessed | tf_op | source)
XLA Modules:
  0.0 78.8 jit_solution(7553695483124584445)
XLA Ops:
  0.6 75.6 %shard_map.59 = (bf16[256,512]{1,0:T(8,128)(2,1)}, f32[256,512]{1,0:T(8,128)}) custom-call(bf16[256,512]{1,0:T(8,128)(2,1)} %bitcast.7, f32[1,512]{1,0:T(1,128)} %bitcast.9, bf16[27,16,512]{2,1,0:T(8,128)(2,1)} %weight_ref.1, bf16[256,512]{1,0:T(8,128)(2,1)} %bitcast.8), custom_call_target="tpu_custom_call" | custom-call | flops 7247757312 | bytes 14155776 | tf_op jit(solution)/shard_map/pallas_call | solution.py:454
  76.2 0.0 copy-start
  76.2 1.7 %copy.8 = bf16[1,2,128,512]{3,2,1,0:T(8,128)(2,1)} copy(bf16[1,2,128,512]{3,2,1,0:T(8,128)(2,1)} %bitcast.6) | data formatting | bytes 524288
  78.0 0.0 copy-done
  78.0 0.8 %copy.9 = f32[1,2,128,512]{3,2,1,0:T(8,128)} copy(f32[1,2,128,512]{3,2,1,0:T(8,128)S(1)} %bitcast.5) | data formatting | bytes 1048576
Async XLA Ops:
  76.2 1.7 %copy-start = (f32[256,512]{1,0:T(8,128)S(1)}, f32[256,512]{1,0:T(8,128)}, u32[]{:S(2)}) copy-start(f32[256,512]{1,0:T(8,128)} %get-tuple-element.5) | copy-start | bytes 1572868

commit v5 on v4

--- a/solution.py
+++ b/solution.py
@@ -159,8 +159,10 @@
     n_b = (taps - n_last_z) // 2
     n_c = taps - n_last_z - n_b
     rounds = n_c
-    line_first = (*range(depth), depth + 1, depth + 3, depth + 4)
-    line_last = (0, 1, *range(2, 2 * depth + 1, 2), 2 * depth + 1)
+    ahead = 3
+    later = max(0, 4 - depth)
+    line_first = (-ahead, *range(depth - 1), depth, depth + 2, depth + 3 + later)
+    line_last = (-ahead, 0, *range(1, 2 * depth, 2), 2 * depth + later)
     kinds = [
         (("z", "x", "y"), 0, n_b, line_first),
         (("z", "y", "x"), n_b, n_c, line_first),
@@ -283,25 +285,15 @@
         a = lax.div(tap, 9)
         b = lax.rem(lax.div(tap, 3), 3)
         e = lax.rem(tap, 3)
-        inner = cells - columns
-
-        def rows_of(out_first, in_first, count):
-            weights = whole[tap].reshape(channels, channels)
-            conv_acc[out_first : out_first + count] += jnp.dot(
-                act_wide[a, e, columns + in_first : columns + in_first + count],
-                weights,
-                preferred_element_type=jnp.float32,
-            )
-            grad_acc[in_first : in_first + count] += lax.dot_general(
-                grad_wide[2 - a, 2 - e, columns + out_first : columns + out_first + count],
-                weights,
-                (((1,), (1,)), ((), ())),
-                preferred_element_type=jnp.float32,
-            )
-
-        pl.when(b == 0)(lambda: rows_of(columns, 0, inner))
-        pl.when(b == 1)(lambda: rows_of(0, 0, cells))
-        pl.when(b == 2)(lambda: rows_of(0, columns, inner))
+        weights = whole[tap].reshape(channels, channels)
+        forward = act_wide[a, e, pl.ds(pl.multiple_of(b * columns, columns), cells)]
+        conv_acc[...] += jnp.dot(forward, weights, preferred_element_type=jnp.float32)
+        back = grad_wide[
+            2 - a, 2 - e, pl.ds(pl.multiple_of((2 - b) * columns, columns), cells)
+        ]
+        grad_acc[...] += lax.dot_general(
+            back, weights, (((1,), (1,)), ((), ())), preferred_element_type=jnp.float32
+        )
 
     def compute(tick):
         for kind in range(len(kinds)):
@@ -332,28 +324,37 @@
         ((me > 1) & (core == 0), halo(act_halo.at[1], me + 1, act_halo.at[0], 3, 4)),
     ]
 
-    advance(0, 0, 1)
-    for fetch in fetches:
-        fetch.wait()
+    for tick in range(-ahead, 0):
+        advance(tick, 0, 1)
+    fetches[0].wait()
     for sends_it, _, this in grad_copies:
         pl.when(sends_it)(this.start)
 
-    latent_wide = latent_ref[...].astype(jnp.float32)
-    gain = gain_ref[...]
     count = cells * group
-    average = group_mean(eight(sums_of(latent_wide)), same_ref, count)[0:1]
-    centred = latent_wide - average
-    spread = group_mean(eight(sums_of(centred * centred)), same_ref, count)[0:1]
-    inverse = lax.rsqrt(spread + epsilon)
-    inverse_ref[...] = inverse
-    normed = centred * inverse
-    normed_ref[...] = normed
-    scaled = normed * gain
-    sigmoid_value = jax.nn.sigmoid(scaled)
-    activated = scaled * sigmoid_value
-    own_act[...] = activated.astype(jnp.bfloat16)
-    for sends_it, _, this in act_copies:
-        pl.when(sends_it)(this.start)
+
+    def normalise():
+        for fetch in fetches[1:]:
+            fetch.wait()
+        latent_wide = latent_ref[...].astype(jnp.float32)
+        gain = gain_ref[...]
+        average = group_mean(eight(sums_of(latent_wide)), same_ref, count)[0:1]
+        centred = latent_wide - average
+        spread = group_mean(eight(sums_of(centred * centred)), same_ref, count)[0:1]
+        inverse = lax.rsqrt(spread + epsilon)
+        inverse_ref[...] = inverse
+        normed = centred * inverse
+        normed_ref[...] = normed
+        scaled = normed * gain
+        sigmoid_value = jax.nn.sigmoid(scaled)
+        slope_ref[...] = sigmoid_value * (1.0 + scaled * (1.0 - sigmoid_value)) * gain
+        own_act[...] = (scaled * sigmoid_value).astype(jnp.bfloat16)
+        for sends_it, _, this in act_copies:
+            pl.when(sends_it)(this.start)
+
+    def widen_own():
+        widen(act_halo[2], act_wide, 2)
+        widen(grad_ref[...], grad_wide, 0)
+
     column = lax.rem(lax.broadcasted_iota(jnp.int32, (cells, channels), 0), columns)
     edge = jnp.zeros((columns, channels), jnp.bfloat16)
 
@@ -366,13 +367,6 @@
             wide[place, e, columns : columns + cells] = part.astype(jnp.bfloat16)
             wide[place, e, columns + cells : 2 * columns + cells] = edge
 
-    def keep_slope():
-        scaled = normed_ref[...] * gain_ref[...]
-        sigmoid_value = jax.nn.sigmoid(scaled)
-        slope_ref[...] = (
-            sigmoid_value * (1.0 + scaled * (1.0 - sigmoid_value)) * gain_ref[...]
-        )
-
     def take(copies, d, buffer, at, wide, place):
         _, gets_it, this = copies[d]
         pl.when(gets_it)(this.wait_recv)
@@ -387,9 +381,8 @@
         widen(buffer[at], wide, place)
 
     jobs = [
-        keep_slope,
-        lambda: widen(act_halo[2], act_wide, 2),
-        lambda: widen(grad_ref[...], grad_wide, 0),
+        normalise,
+        widen_own,
         lambda: take(grad_copies, 0, grad_halo, 0, grad_wide, 1),
         lambda: take(act_copies, 0, act_halo, 1, act_wide, 1),
         lambda: take(grad_copies, 1, grad_halo, 1, grad_wide, 2),
@@ -404,7 +397,7 @@
 
     first_use = min(entry[3][stages] for entry in kinds)
     last_use = max(entry[3][stages] for entry in kinds)
-    lax.fori_loop(1, first_use, early, 0)
+    lax.fori_loop(0, first_use, early, 0)
 
     def late(tick, carry):
         advance(tick, 0, stages + 1)

time: 79 us -> 81.5 us (1.032)
  Pallas kernels: 75.6 us -> 78.1 us
    pallas_call x1, Pallas kernels: 75.6 us -> 78.1 us  [fused(): pl.pallas_call(functools.partial(block_kernel, n, columns), out_shape=(ja...]
where the time goes in v5:
time: 81.5 us; the launch traced here: 81.3 us
  Pallas kernels  78.1 us (96%)
  local copies, waits for them, and re-layouts  2.52 us (3%)
    pallas_call x1, Pallas kernels, fused(): pl.pallas_call(functools.partial(block_kernel, n, columns), out_shape=(ja...  78.1 us
    unnamed x4, local copies, waits for them, and re-layouts  2.52 us

profile of v5, /device:TPU:0, one launch (start us, length us, event | category | flops | bytes accessed | tf_op | source)
XLA Modules:
  0.0 81.3 jit_solution(1417181888076689517)
XLA Ops:
  0.6 78.1 %shard_map.59 = (bf16[256,512]{1,0:T(8,128)(2,1)}, f32[256,512]{1,0:T(8,128)}) custom-call(bf16[256,512]{1,0:T(8,128)(2,1)} %bitcast.7, f32[1,512]{1,0:T(1,128)} %bitcast.9, bf16[27,16,512]{2,1,0:T(8,128)(2,1)} %weight_ref.1, bf16[256,512]{1,0:T(8,128)(2,1)} %bitcast.8), custom_call_target="tpu_custom_call" | custom-call | flops 7247757312 | bytes 14155776 | tf_op jit(solution)/shard_map/pallas_call | solution.py:447
  78.8 0.0 copy-start
  78.8 1.7 %copy.8 = bf16[1,2,128,512]{3,2,1,0:T(8,128)(2,1)} copy(bf16[1,2,128,512]{3,2,1,0:T(8,128)(2,1)} %bitcast.6) | data formatting | bytes 524288
  80.5 0.0 copy-done
  80.5 0.8 copy.9
Async XLA Ops:
  78.8 1.7 %copy-start = (f32[256,512]{1,0:T(8,128)S(1)}, f32[256,512]{1,0:T(8,128)}, u32[]{:S(2)}) copy-start(f32[256,512]{1,0:T(8,128)} %get-tuple-element.5) | copy-start | bytes 1572868
